TPU v7x, 256 devices: a whole 4x4x8 slice. The times are simulated.
256 devices in a mesh: expert: 32 (over z, x), dp: 8 (over y, core).
Axes of the slice: x: 4, y: 4, z: 8, core: 2. Of those that a mesh axis runs over, the one named last changes fastest.
Arguments:
- tokens: bfloat16 [3072, 4096], P('expert', 'dp'), may hold values from -6 to 6
- route_weight: float32 [3072, 8], P('expert'), may hold values from 0.05 to 0.25
- route_expert: int32 [3072, 8], P('expert'), may hold values from 0 to 31, all different within a row; in each aligned block of 96 rows (0 to 95, 96 to 191, ...) at most 32 rows name the same one
- cotangent: bfloat16 [3072, 4096], P('expert', 'dp'), may hold values from -6 to 6
- gate_quant: bfloat16 [32, 4096, 1024], P('expert', None, 'dp'), may hold values from -0.09375 to 0.09375
- up_quant: bfloat16 [32, 4096, 1024], P('expert', None, 'dp'), may hold values from -0.09375 to 0.09375
- gate_scale: float32 [32, 32, 8], P('expert', None, 'dp'), may hold values from 0.5 to 2
- up_scale: float32 [32, 32, 8], P('expert', None, 'dp'), may hold values from 0.5 to 2
- down_quant: bfloat16 [32, 1024, 4096], P('expert', None, 'dp'), may hold values from -0.1875 to 0.1875
- down_scale: float32 [32, 8, 32], P('expert', None, 'dp'), may hold values from 0.5 to 2
- first_moment: float32 [32, 1024, 4096], P('expert', None, 'dp'), may hold values from -6 to 6
- second_moment: float32 [32, 1024, 4096], P('expert', None, 'dp'), may hold values from 0.5 to 8
- old_expert: int32 [32], replicated, may hold values from 0 to 31, each once
- new_holder: int32 [32], replicated, may hold values from 0 to 31, each once
Outputs:
- mixed: bfloat16 [3072, 4096], P('expert', 'dp')
- new_down: bfloat16 [32, 1024, 4096], P('expert', None, 'dp')
- new_first: float32 [32, 1024, 4096], P('expert', None, 'dp')
- new_second: float32 [32, 1024, 4096], P('expert', None, 'dp')
Inputs may be any that keep to these rules, and one draw needn't show every extreme that they name: `route_expert`: within each aligned block of 96 tokens (the tokens of one index of expert) no expert is named by more than 32 routes, a bound that some block reaches; a token names 8 different experts. `old_expert`: A permutation of the experts. `new_holder`: A permutation of the indices of expert.
All inputs are finite; a program needn't handle non-finite values.
Results may differ from a plain program's by a relative error of at most 0.0076.
Values may be sent and summed in bfloat16 or wider, within the bound.
A program may use at most 128 MiB of HBM per device.

v0:
```python
import jax
import jax.numpy as jnp
from jax import lax
from jax.sharding import PartitionSpec as P

QB = 128
beta_first = 0.9
beta_second = 0.95
adam_eps = 1e-08
learn_rate = 0.003
decay_rate = 0.1
step_count = 20


def dequantize(quant, scale):
    tiled = jnp.repeat(jnp.repeat(scale, QB, axis=0), QB, axis=1)
    return quant.astype(jnp.float32) * tiled


def adam_step(master, grad, first, second):
    first_new = beta_first * first + (1.0 - beta_first) * grad
    second_new = beta_second * second + (1.0 - beta_second) * grad * grad
    fix_first = 1.0 - beta_first**step_count
    fix_second = 1.0 - beta_second**step_count
    update = first_new / fix_first / (jnp.sqrt(second_new / fix_second) + adam_eps)
    fresh = (master - learn_rate * (update + decay_rate * master)).astype(jnp.bfloat16)
    return (fresh, first_new, second_new)


def holder_tables(old_expert, new_holder):
    number = old_expert.shape[0]
    labels = jnp.arange(number, dtype=jnp.int32)
    holds = (old_expert[:, None] == labels[None, :]).astype(jnp.int32)
    old_device = jnp.sum(holds * labels[:, None], axis=0)
    new_device = jnp.sum(holds * new_holder[:, None], axis=0)
    takes = (new_holder[:, None] == labels[None, :]).astype(jnp.int32)
    giver = jnp.sum(takes * labels[:, None], axis=0)
    return (old_device, new_device, giver)


def pack_rows(arrays, number):
    lines = []
    for array_item in arrays:
        line = array_item.reshape(-1)
        lines.append(line.reshape(number, -1))
    return jnp.concatenate(lines, axis=1)


def unpack_rows(packed, arrays):
    number = packed.shape[0]
    result = []
    offset = 0
    for array_item in arrays:
        span_cols = -(-array_item.size // number)
        block_rows = packed[:, offset : offset + span_cols]
        result.append(block_rows.reshape(-1).reshape(array_item.shape))
        offset = offset + span_cols
    return tuple(result)


def move_weights(arrays, giver):
    packed = pack_rows(arrays, giver.shape[0])
    spread = lax.all_to_all(packed, "expert", split_axis=0, concat_axis=0, tiled=True)
    settled = lax.all_to_all(
        jnp.take(spread, giver, axis=0), "expert", split_axis=0, concat_axis=0, tiled=True
    )
    return unpack_rows(settled, arrays)


def move_state(arrays, giver):
    packed = pack_rows(arrays, giver.shape[0])
    spread = lax.all_to_all(packed, "expert", split_axis=0, concat_axis=0, tiled=True)
    settled = lax.all_to_all(
        jnp.take(spread, giver, axis=0), "expert", split_axis=0, concat_axis=0, tiled=True
    )
    return unpack_rows(settled, arrays)


def plan_slots(route_expert, target_of, number, capacity):
    route_total = route_expert.shape[0] * route_expert.shape[1]
    flat_expert = route_expert.reshape(-1)
    labels = jnp.arange(number, dtype=jnp.int32)
    pick = (flat_expert[:, None] == labels[None, :]).astype(jnp.int32)
    target = jnp.sum(pick * target_of[None, :], axis=1)
    onehot = (target[:, None] == labels[None, :]).astype(jnp.int32)
    earlier = jnp.cumsum(onehot, axis=0) - onehot
    slot_index = jnp.sum(earlier * onehot, axis=1)
    route_place = target * capacity + slot_index
    slot_route = (
        jnp.full((number * capacity,), -1, jnp.int32)
        .at[route_place]
        .set(jnp.arange(route_total, dtype=jnp.int32))
    )
    return (route_place, slot_route)


def per_device(
    tokens,
    route_weight,
    route_expert,
    cotangent,
    gate_quant,
    up_quant,
    gate_scale,
    up_scale,
    down_quant,
    down_scale,
    first_moment,
    second_moment,
    old_expert,
    new_holder,
):
    number = lax.axis_size("expert")
    tok_rows, top_count = route_expert.shape
    model_width = gate_quant.shape[1]
    column_width = cotangent.shape[1]
    capacity = min(tok_rows, tok_rows * top_count // number * 4 // 3)
    old_device, new_device, giver = holder_tables(old_expert, new_holder)
    gate_quant, up_quant, down_quant = move_weights((gate_quant, up_quant, down_quant), giver)
    gate_scale, up_scale, down_scale, first_moment, second_moment = move_state(
        (gate_scale, up_scale, down_scale, first_moment, second_moment), giver
    )
    route_place, slot_route = plan_slots(route_expert, new_device, number, capacity)
    live_rows = slot_route >= 0
    safe_route = jnp.maximum(slot_route, 0)
    token_ids = safe_route // top_count
    weight_rows = jnp.where(
        live_rows, jnp.take(route_weight.reshape(-1), safe_route), jnp.float32(0.0)
    )
    back_rows = (
        weight_rows[:, None] * jnp.take(cotangent, token_ids, axis=0).astype(jnp.float32)
    ).astype(jnp.bfloat16)
    back_send = back_rows.reshape(number, capacity, column_width)
    whole_tokens = lax.all_gather(tokens, "dp", axis=1, tiled=True)
    sent_rows = jnp.take(whole_tokens, token_ids, axis=0).reshape(number, capacity, model_width)
    arrived, back_in = (
        lax.all_to_all(sent_rows, "expert", split_axis=0, concat_axis=0, tiled=True),
        lax.all_to_all(back_send, "expert", split_axis=0, concat_axis=0, tiled=True),
    )
    rows_in = arrived.reshape(-1, model_width)
    back_in = back_in.reshape(-1, column_width)
    gate_w = dequantize(gate_quant[0], gate_scale[0]).astype(jnp.bfloat16)
    up_w = dequantize(up_quant[0], up_scale[0]).astype(jnp.bfloat16)
    master = dequantize(down_quant[0], down_scale[0])
    down_w = master.astype(jnp.bfloat16)
    gate_val = jnp.dot(rows_in, gate_w, preferred_element_type=jnp.float32)
    up_val = jnp.dot(rows_in, up_w, preferred_element_type=jnp.float32)
    hidden_part = (jax.nn.silu(gate_val) * up_val).astype(jnp.bfloat16)
    hidden_full = lax.all_gather(hidden_part, "dp", axis=1, tiled=True)
    out_total = jnp.dot(hidden_full, down_w, preferred_element_type=jnp.float32)
    grad_total = lax.dot_general(
        hidden_full, back_in, (((0,), (0,)), ((), ())), preferred_element_type=jnp.float32
    )
    out_rows = out_total.astype(jnp.bfloat16).reshape(number, capacity, column_width)
    returned = lax.all_to_all(out_rows, "expert", split_axis=0, concat_axis=0, tiled=True).reshape(
        -1, column_width
    )
    picked = (
        jnp.take(returned, route_place, axis=0)
        .reshape(tok_rows, top_count, column_width)
        .astype(jnp.float32)
    )
    mixed = jnp.sum(picked * route_weight[:, :, None], axis=1).astype(jnp.bfloat16)
    fresh, first_new, second_new = adam_step(master, grad_total, first_moment[0], second_moment[0])
    fresh = fresh[None]
    first_new = first_new[None]
    second_new = second_new[None]
    return (mixed, fresh, first_new, second_new)


def solution(mesh):
    in_specs = (
        P("expert", "dp"),
        P("expert", None),
        P("expert", None),
        P("expert", "dp"),
        P("expert", None, "dp"),
        P("expert", None, "dp"),
        P("expert", None, "dp"),
        P("expert", None, "dp"),
        P("expert", None, "dp"),
        P("expert", None, "dp"),
        P("expert", None, "dp"),
        P("expert", None, "dp"),
        P(),
        P(),
    )
    out_specs = (
        P("expert", "dp"),
        P("expert", None, "dp"),
        P("expert", None, "dp"),
        P("expert", None, "dp"),
    )
    return jax.shard_map(
        per_device, mesh=mesh, in_specs=in_specs, out_specs=out_specs, check_vma=False
    )
```

profile of v0, /device:TPU:2, one launch (start us, length us, event | category | flops | bytes accessed | tf_op | source)
XLA Modules:
  0.0 698.2 jit_solution(656383670032208674)
XLA Ops:
  7.2 2.4 reshape_reshape.24
  9.7 1.3 reshape_reshape.25
  10.9 1.3 reshape_reshape.26
  12.2 2.0 maximum_bitcast_fusion
  14.7 3.8 reduce.10
  18.5 5.4 reshape.303
  23.9 11.8 %all-to-all-start.1 = ((bf16[32,2,24576]{2,1,0:T(2,128)(2,1)}), bf16[32,2,24576]{2,1,0:T(2,128)(2,1)S(1)}, u32[]{:S(2)}, u32[]{:S(2)}) async-start(bf16[32,2,24576]{2,1,0:T(2,128)(2,1)} %reshape.303), calls=%async_computation.1 | async-start | bytes 6291456 | tf_op jit(solution)/shard_map/all_to_all | solution.py:63
  36.0 2.7 reshape_reshape.30
  38.7 2.7 reshape_reshape.31
  41.5 1.3 dynamic-update-slice
  42.8 1.4 dynamic-update-slice.1
  44.2 1.4 dynamic-update-slice.2
  45.6 9.3 %dynamic-update-slice.3 = f32[32,32771]{1,0:T(8,128)} dynamic-update-slice(f32[32,32771]{1,0:T(8,128)} %dynamic-update-slice.2, f32[32,16384]{1,0:T(8,128)} %reshape_reshape.30, s32[]{} %constant.150, s32[]{} %constant.153) | dynamic-update-slice | bytes 4194308
  54.9 8.7 %dynamic-update-slice.4 = f32[32,32771]{1,0:T(8,128)} dynamic-update-slice(f32[32,32771]{1,0:T(8,128)} %dynamic-update-slice.3, f32[32,16384]{1,0:T(8,128)} %reshape_reshape.31, s32[]{} %constant.150, s32[]{} %constant.154) | dynamic-update-slice | bytes 4194308 | tf_op jit(solution)/shard_map/concatenate | solution.py:46
  63.5 9.8 %all_to_all.43 = f32[32,1,32771]{2,1,0:T(1,128)} reshape(f32[32,32771]{1,0:T(8,128)} %dynamic-update-slice.4) | data formatting | bytes 8389376 | tf_op jit(solution)/shard_map/all_to_all | solution.py:72
  73.5 33.4 %all-to-all-done.1 = bf16[32,2,24576]{2,1,0:T(2,128)(2,1)S(1)} async-done(((bf16[32,2,24576]{2,1,0:T(2,128)(2,1)}), bf16[32,2,24576]{2,1,0:T(2,128)(2,1)S(1)}, u32[]{:S(2)}, u32[]{:S(2)}) %all-to-all-start.1) | async-done | bytes 3145760 | tf_op jit(solution)/shard_map/all_to_all | solution.py:63
  106.9 7.8 %all-to-all-start.3 = ((f32[32,1,32771]{2,1,0:T(1,128)}), f32[32,1,32771]{2,1,0:T(1,128)}, u32[]{:S(2)}, u32[]{:S(2)}) async-start(f32[32,1,32771]{2,1,0:T(1,128)} %all_to_all.43), calls=%async_computation.3 | async-start | bytes 8421376 | tf_op jit(solution)/shard_map/all_to_all | solution.py:72
  114.7 12.4 %reshape.304 = bf16[32,1,49152]{2,1,0:T(2,128)(2,1)} reshape(bf16[32,2,24576]{2,1,0:T(2,128)(2,1)S(1)} %all-to-all-done.1) | data formatting | bytes 6291456
  127.2 6.2 copy.83
  133.4 4.3 gather_fusion.1
  137.7 2.3 bitcast_select_fusion.1
  139.9 3.7 reduce.11
  143.7 5.4 reshape.305
  149.1 59.0 %all-to-all-done.3 = f32[32,1,32771]{2,1,0:T(1,128)} async-done(((f32[32,1,32771]{2,1,0:T(1,128)}), f32[32,1,32771]{2,1,0:T(1,128)}, u32[]{:S(2)}, u32[]{:S(2)}) %all-to-all-start.3) | async-done | bytes 4194720 | tf_op jit(solution)/shard_map/all_to_all | solution.py:72
  208.1 8.3 %all-to-all-start.2 = ((bf16[32,2,24576]{2,1,0:T(2,128)(2,1)}), bf16[32,2,24576]{2,1,0:T(2,128)(2,1)}, u32[]{:S(2)}, u32[]{:S(2)}) async-start(bf16[32,2,24576]{2,1,0:T(2,128)(2,1)} %reshape.305), calls=%async_computation.2 | async-start | bytes 6291456 | tf_op jit(solution)/shard_map/all_to_all | solution.py:64
  216.5 4.4 copy.81
  220.9 7.6 %gather_fusion.2 = f32[32,32771]{1,0:T(8,128)} fusion(f32[32,32771]{1,0:T(8,128)} %bitcast.77, s32[1024]{0:T(1024)S(1)} %pad_clamp_fusion.1), kind=kCustom, calls=%fused_computation.2 | custom fusion | bytes 8389504 | tf_op jit(solution)/shard_map/jit(_take)/gather | solution.py:74
  228.5 2.5 bitcast_select_fusion
  231.0 6.3 copy.60
  237.3 50.3 %all-to-all-done.2 = bf16[32,2,24576]{2,1,0:T(2,128)(2,1)} async-done(((bf16[32,2,24576]{2,1,0:T(2,128)(2,1)}), bf16[32,2,24576]{2,1,0:T(2,128)(2,1)}, u32[]{:S(2)}, u32[]{:S(2)}) %all-to-all-start.2) | async-done | bytes 3145760 | tf_op jit(solution)/shard_map/all_to_all | solution.py:64
  287.6 7.4 %all-to-all-start.4 = ((f32[32,1,32771]{2,1,0:T(1,128)}), f32[32,1,32771]{2,1,0:T(1,128)}, u32[]{:S(2)}, u32[]{:S(2)}) async-start(f32[32,1,32771]{2,1,0:T(1,128)} %copy.60), calls=%async_computation.4 | async-start | bytes 8421376 | tf_op jit(solution)/shard_map/all_to_all | solution.py:73
  295.3 1.7 reduce-window.6
  297.5 3.4 scatter_custom_fusion
  301.0 14.1 %all_gather.6 = bf16[96,4096]{1,0:T(8,128)(2,1)S(1)} all-gather(bf16[96,512]{1,0:T(8,128)(2,1)S(1)} %copy-done.7), channel_id=1, replica_groups=mesh['expert'=32,'dp'=8] {'dp'}, dimensions={1}, use_global_device_ids=true | all-gather | bytes 884736 | tf_op jit(solution)/shard_map/all_gather | solution.py:134
  315.1 7.8 %gather_fusion = bf16[1024,4096]{1,0:T(8,128)(2,1)} fusion(bf16[96,4096]{1,0:T(8,128)(2,1)S(1)} %all_gather.6, s32[1024]{0:T(1024)S(1)} %get-tuple-element.17), kind=kCustom, calls=%fused_computation | custom fusion | bytes 16781312 | tf_op jit(solution)/shard_map/jit(_take)/gather | solution.py:135
  322.9 7.4 %broadcast_select_fusion = bf16[32,32,4096]{2,1,0:T(8,128)(2,1)} fusion(bf16[32,32,4096]{2,1,0:T(8,128)(2,1)} %bitcast.80, pred[32,32]{1,0:T(8,128)(4,1)S(1)} %broadcast_in_dim.103), kind=kLoop, calls=%fused_computation.7 | loop fusion | flops 4194304 | bytes 16778240 | tf_op jit(solution)/shard_map/jit(_take)/select_n | solution.py:135
  330.3 58.3 %all-to-all-done.4 = f32[32,1,32771]{2,1,0:T(1,128)} async-done(((f32[32,1,32771]{2,1,0:T(1,128)}), f32[32,1,32771]{2,1,0:T(1,128)}, u32[]{:S(2)}, u32[]{:S(2)}) %all-to-all-start.4) | async-done | bytes 4194720 | tf_op jit(solution)/shard_map/all_to_all | solution.py:73
  388.7 7.7 %all-to-all-start = ((bf16[32,32,4096]{2,1,0:T(8,128)(2,1)}), bf16[32,32,4096]{2,1,0:T(8,128)(2,1)}, u32[]{:S(2)}, u32[]{:S(2)}) async-start(bf16[32,32,4096]{2,1,0:T(8,128)(2,1)} %broadcast_select_fusion), calls=%async_computation | async-start | bytes 16777216 | tf_op jit(solution)/shard_map/all_to_all | solution.py:137
  396.6 4.5 gather_fusion.4
  401.2 4.0 gather_fusion.5
  405.2 1.3 multiply_convert_fusion
  406.5 18.9 %reshape.306 = bf16[32,1,49152]{2,1,0:T(2,128)(2,1)} reshape(bf16[32,2,24576]{2,1,0:T(2,128)(2,1)} %all-to-all-done.2) | data formatting | bytes 6291456
  425.4 6.2 copy.82
  431.7 2.5 copy.80
  434.4 2.2 multiply_convert_fusion.2
  436.7 2.3 convert_element_type.66
  439.1 2.3 convert_element_type.69
  441.4 145.2 %all-to-all-done = bf16[32,32,4096]{2,1,0:T(8,128)(2,1)} async-done(((bf16[32,32,4096]{2,1,0:T(8,128)(2,1)}), bf16[32,32,4096]{2,1,0:T(8,128)(2,1)}, u32[]{:S(2)}, u32[]{:S(2)}) %all-to-all-start) | async-done | bytes 8388640 | tf_op jit(solution)/shard_map/all_to_all | solution.py:137
  586.6 13.2 %all-to-all-start.6 = ((bf16[32,32,512]{2,1,0:T(8,128)(2,1)}), bf16[32,32,512]{2,1,0:T(8,128)(2,1)}, u32[]{:S(2)}, u32[]{:S(2)}) async-start(bf16[32,32,512]{2,1,0:T(8,128)(2,1)} %multiply_convert_fusion), calls=%async_computation.6 | async-start | bytes 2097152 | tf_op jit(solution)/shard_map/all_to_all | solution.py:138
  600.1 6.0 fusion.15
  606.1 6.4 fusion.1
  612.6 1.5 slice_convert_fusion
  614.0 1.7 reshape.234
  615.9 27.8 %all-gather.2.cloned.1.call-done = bf16[1024,1024]{1,0:T(8,128)(2,1)} async-done(((bf16[1024,128]{1,0:T(8,128)(2,1)}), bf16[1024,1024]{1,0:T(8,128)(2,1)}) %all-gather.2.cloned.1.call-update) | async-done | bytes 2097168 | tf_op jit(solution)/shard_map/all_gather | solution.py:149
  644.9 1.3 copy-done.2
  646.3 2.3 convolution_convert_fusion
  648.5 10.1 %all-to-all-start.5 = ((bf16[32,32,512]{2,1,0:T(8,128)(2,1)}), bf16[32,32,512]{2,1,0:T(8,128)(2,1)S(1)}, u32[]{:S(2)}, u32[]{:S(2)}) async-start(bf16[32,32,512]{2,1,0:T(8,128)(2,1)} %bitcast.12), calls=%async_computation.5 | async-start | bytes 2097152 | tf_op jit(solution)/shard_map/all_to_all | solution.py:155
  658.7 4.7 slice_multiply_fusion
  663.4 2.7 mul.139
  666.1 1.5 mul.146
  667.6 9.3 %fusion.5 = (f32[1,1024,512]{2,1,0:T(8,128)}, bf16[1,1024,512]{2,1,0:T(8,128)(2,1)}, f32[1,1024,512]{2,1,0:T(8,128)}) fusion(f32[1024,512]{1,0:T(8,128)} %mul.146, f32[1024,512]{1,0:T(8,128)} %mul.139, f32[1024,512]{1,0:T(8,128)} %copy-done.3, f32[128,8,4,128]{3,2,1,0:T(4,128)} %bitcast.87, bf16[1024,1024]{1,0:T(8,128)(2,1)} %all-gather.2.cloned.1.call-done, ...), kind=kOutput, calls=%fused_computation.34 | convolution fusion | flops 1081606144 | bytes 16777216 | tf_op jit(solution)/shard_map/dot_general | solution.py:151
  676.9 10.2 %all-to-all-done.5 = bf16[32,32,512]{2,1,0:T(8,128)(2,1)S(1)} async-done(((bf16[32,32,512]{2,1,0:T(8,128)(2,1)}), bf16[32,32,512]{2,1,0:T(8,128)(2,1)S(1)}, u32[]{:S(2)}, u32[]{:S(2)}) %all-to-all-start.5) | async-done | bytes 1048608 | tf_op jit(solution)/shard_map/all_to_all | solution.py:155
  687.2 2.7 gather_fusion.3
  689.8 1.3 multiply_reduce_fusion
  (68 shorter events, 4.3 us)
Async XLA Ops:
  7.2 394.1 %copy-start = (bf16[96,512]{1,0:T(8,128)(2,1)S(1)}, bf16[96,512]{1,0:T(8,128)(2,1)}, u32[]{:S(2)}) copy-start(bf16[96,512]{1,0:T(8,128)(2,1)} %param.17) | copy-start | bytes 294916
  7.2 2.5 copy-start.4
  7.2 3.7 copy-start.5
  23.9 11.8 %copy-start.11 = (f32[1,32,1]{1,2,0:T(1,128)S(1)}, f32[1,32,1]{1,2,0:T(1,128)}, u32[]{:S(2)}) copy-start(f32[1,32,1]{1,2,0:T(1,128)} %param.20) | copy-start | bytes 388
  23.9 11.9 %copy-start.12 = (f32[1,32,1]{1,2,0:T(1,128)S(1)}, f32[1,32,1]{1,2,0:T(1,128)}, u32[]{:S(2)}) copy-start(f32[1,32,1]{1,2,0:T(1,128)} %param.21) | copy-start | bytes 388
  23.9 12.0 %copy-start.10 = (f32[1,8,4]{1,2,0:T(4,128)S(1)}, f32[1,8,4]{1,2,0:T(4,128)}, u32[]{:S(2)}) copy-start(f32[1,8,4]{1,2,0:T(4,128)} %param.23) | copy-start | bytes 388
  23.9 83.0 %all-to-all-start.1 = ((bf16[32,2,24576]{2,1,0:T(2,128)(2,1)}), bf16[32,2,24576]{2,1,0:T(2,128)(2,1)S(1)}, u32[]{:S(2)}, u32[]{:S(2)}) async-start(bf16[32,2,24576]{2,1,0:T(2,128)(2,1)} %reshape.303), calls=%async_computation.1 | async-start | bytes 6291456 | tf_op jit(solution)/shard_map/all_to_all | solution.py:63
  63.5 9.8 %copy-start.13 = (s32[32]{0:T(128)S(1)}, s32[32]{0:T(128)}, u32[]{:S(2)}) copy-start(s32[32]{0:T(128)} %param.27) | copy-start | bytes 388
  63.5 9.8 %copy-start.14 = (s32[32]{0:T(128)S(1)}, s32[32]{0:T(128)}, u32[]{:S(2)}) copy-start(s32[32]{0:T(128)} %param.26) | copy-start | bytes 388
  106.9 101.2 %all-to-all-start.3 = ((f32[32,1,32771]{2,1,0:T(1,128)}), f32[32,1,32771]{2,1,0:T(1,128)}, u32[]{:S(2)}, u32[]{:S(2)}) async-start(f32[32,1,32771]{2,1,0:T(1,128)} %all_to_all.43), calls=%async_computation.3 | async-start | bytes 8421376 | tf_op jit(solution)/shard_map/all_to_all | solution.py:72
  208.1 79.5 %all-to-all-start.2 = ((bf16[32,2,24576]{2,1,0:T(2,128)(2,1)}), bf16[32,2,24576]{2,1,0:T(2,128)(2,1)}, u32[]{:S(2)}, u32[]{:S(2)}) async-start(bf16[32,2,24576]{2,1,0:T(2,128)(2,1)} %reshape.305), calls=%async_computation.2 | async-start | bytes 6291456 | tf_op jit(solution)/shard_map/all_to_all | solution.py:64
  237.3 57.7 %copy-start.8 = (s32[96,8]{0,1:T(8,128)S(1)}, s32[96,8]{0,1:T(8,128)}, u32[]{:S(2)}) copy-start(s32[96,8]{0,1:T(8,128)} %param.16) | copy-start | bytes 9220
  237.3 63.7 %copy-start.7 = (bf16[96,512]{1,0:T(8,128)(2,1)S(1)}, bf16[96,512]{1,0:T(8,128)(2,1)}, u32[]{:S(2)}) copy-start(bf16[96,512]{1,0:T(8,128)(2,1)} %param.14) | copy-start | bytes 294916
  287.6 101.0 %all-to-all-start.4 = ((f32[32,1,32771]{2,1,0:T(1,128)}), f32[32,1,32771]{2,1,0:T(1,128)}, u32[]{:S(2)}, u32[]{:S(2)}) async-start(f32[32,1,32771]{2,1,0:T(1,128)} %copy.60), calls=%async_computation.4 | async-start | bytes 8421376 | tf_op jit(solution)/shard_map/all_to_all | solution.py:73
  330.3 66.1 %copy-start.9 = (f32[96,8]{0,1:T(8,128)S(1)}, f32[96,8]{0,1:T(8,128)}, u32[]{:S(2)}) copy-start(f32[96,8]{0,1:T(8,128)} %param.15) | copy-start | bytes 9220
  388.7 198.0 %all-to-all-start = ((bf16[32,32,4096]{2,1,0:T(8,128)(2,1)}), bf16[32,32,4096]{2,1,0:T(8,128)(2,1)}, u32[]{:S(2)}, u32[]{:S(2)}) async-start(bf16[32,32,4096]{2,1,0:T(8,128)(2,1)} %broadcast_select_fusion), calls=%async_computation | async-start | bytes 16777216 | tf_op jit(solution)/shard_map/all_to_all | solution.py:137
  434.1 2.6 copy-start.1
  586.6 61.9 %all-to-all-start.6 = ((bf16[32,32,512]{2,1,0:T(8,128)(2,1)}), bf16[32,32,512]{2,1,0:T(8,128)(2,1)}, u32[]{:S(2)}, u32[]{:S(2)}) async-start(bf16[32,32,512]{2,1,0:T(8,128)(2,1)} %multiply_convert_fusion), calls=%async_computation.6 | async-start | bytes 2097152 | tf_op jit(solution)/shard_map/all_to_all | solution.py:138
  599.8 43.9 %all-gather.2.cloned.1.call-start = ((), (), s32[]{:S(2)}) async-start(), calls=%async_computation.7 | async-start | bytes 2359296 | tf_op jit(solution)/shard_map/all_gather | solution.py:149
  600.1 6.0 copy-start.6
  615.8 32.8 %copy-start.3 = (f32[1024,512]{1,0:T(8,128)}, f32[1024,512]{1,0:T(8,128)S(1)}, u32[]{:S(2)}) copy-start(f32[1024,512]{1,0:T(8,128)S(1)} %reshape.234) | copy-start | bytes 6291460
  643.6 2.6 copy-start.15
  644.9 1.3 copy-start.2
  648.5 38.6 %all-to-all-start.5 = ((bf16[32,32,512]{2,1,0:T(8,128)(2,1)}), bf16[32,32,512]{2,1,0:T(8,128)(2,1)S(1)}, u32[]{:S(2)}, u32[]{:S(2)}) async-start(bf16[32,32,512]{2,1,0:T(8,128)(2,1)} %bitcast.12), calls=%async_computation.5 | async-start | bytes 2097152 | tf_op jit(solution)/shard_map/all_to_all | solution.py:155
Sparse Core Ops, SparseCore 0:
  612.7 30.9 all-gather.1
where the time goes:
time: 706 us; the launch traced here: 698 us
  waiting for transfers between devices  384 us (54%)
  local copies, waits for them, and re-layouts  160 us (23%)
  starting transfers between devices  66.5 us (9%)
  other arithmetic  34.7 us (5%)
  matrix products  24 us (3%)
  between operations  14.6 us (2%)
  blocking collectives  14.1 us (2%)
    all_to_all x1, waiting for transfers between devices, per_device(): lax.all_to_all(sent_rows, 'expert', split_axis=0, concat_axis=0, tiled=True)  145 us
    unnamed x47, local copies, waits for them, and re-layouts  76.8 us
    all_to_all x1, waiting for transfers between devices, move_state(): lax.all_to_all(packed, 'expert', split_axis=0, concat_axis=0, tiled=True)  59 us
    all_to_all x1, waiting for transfers between devices, move_state(): lax.all_to_all(jnp.take(spread, giver, axis=0), 'expert', split_axis=0, c...  58.3 us
    all_to_all x1, waiting for transfers between devices, move_weights(): lax.all_to_all(jnp.take(spread, giver, axis=0), 'expert', split_axis=0, c...  50.3 us
    all_to_all x1, waiting for transfers between devices, move_weights(): lax.all_to_all(packed, 'expert', split_axis=0, concat_axis=0, tiled=True)  33.4 us
    all_gather x1, waiting for transfers between devices, per_device(): hidden_full = lax.all_gather(hidden_part, 'dp', axis=1, tiled=True)  27.8 us
  transfers between devices with their start and end apart: 8, of which 7 were waited for; matrix products, arithmetic and copies ran while one was open for 27% of the time, Pallas kernels for 0%

commit v1 on v0

--- a/solution.py
+++ b/solution.py
@@ -131,7 +131,12 @@
         weight_rows[:, None] * jnp.take(cotangent, token_ids, axis=0).astype(jnp.float32)
     ).astype(jnp.bfloat16)
     back_send = back_rows.reshape(number, capacity, column_width)
-    whole_tokens = lax.all_gather(tokens, "dp", axis=1, tiled=True)
+    ring = [tokens]
+    for hop in range(7):
+        ring.append(lax.ppermute(ring[-1], "dp", [(dev, (dev + 1) % 8) for dev in range(8)]))
+    whole_tokens = jnp.roll(
+        jnp.concatenate(ring[::-1], axis=1), (lax.axis_index("dp") + 1) * ring[0].shape[1], axis=1
+    )
     sent_rows = jnp.take(whole_tokens, token_ids, axis=0).reshape(number, capacity, model_width)
     arrived, back_in = (
         lax.all_to_all(sent_rows, "expert", split_axis=0, concat_axis=0, tiled=True),

time: 706 us -> 706 us (level)
  blocking collectives: 14.1 us -> 0 us
  waiting for transfers between devices: 384 us -> 398 us
    ppermute x0 -> x7, waiting for transfers between devices: none -> 30.6 us  [per_device(): lax.ppermute(ring[-1], 'dp', [(dev, (dev + 1) % 8) for dev in range(8)])]
    all_to_all x1, waiting for transfers between devices: 58.3 us -> 41.3 us  [move_state(): lax.all_to_all(jnp.take(spread, giver, axis=0), 'expert', split_axis=0, c...]
    all_gather x1 -> x0, blocking collectives: 14.1 us -> none  [per_device(): whole_tokens = lax.all_gather(tokens, 'dp', axis=1, tiled=True)]
    unnamed x47 -> x62, local copies, waits for them, and re-layouts: 76.8 us -> 77 us
  transfers between devices with their start and end apart: 8 -> 15, of which waited for: 7 -> 14; matrix products, arithmetic and copies ran while one was open for 27% -> 27% of each run, Pallas kernels for 0% -> 0%
where the time goes in v1:
time: 706 us; the launch traced here: 698 us
  waiting for transfers between devices  398 us (56%)
  local copies, waits for them, and re-layouts  160 us (23%)
  starting transfers between devices  66.5 us (9%)
  other arithmetic  34.7 us (5%)
  matrix products  24.1 us (3%)
  between operations  14.8 us (2%)
    all_to_all x1, waiting for transfers between devices, per_device(): lax.all_to_all(sent_rows, 'expert', split_axis=0, concat_axis=0, tiled=True)  145 us
    unnamed x62, local copies, waits for them, and re-layouts  77 us
    all_to_all x1, waiting for transfers between devices, move_state(): lax.all_to_all(packed, 'expert', split_axis=0, concat_axis=0, tiled=True)  59 us
    all_to_all x1, waiting for transfers between devices, move_weights(): lax.all_to_all(jnp.take(spread, giver, axis=0), 'expert', split_axis=0, c...  50.3 us
    all_to_all x1, waiting for transfers between devices, move_state(): lax.all_to_all(jnp.take(spread, giver, axis=0), 'expert', split_axis=0, c...  41.3 us
    all_to_all x1, waiting for transfers between devices, move_weights(): lax.all_to_all(packed, 'expert', split_axis=0, concat_axis=0, tiled=True)  33.4 us
    ppermute x7, waiting for transfers between devices, per_device(): lax.ppermute(ring[-1], 'dp', [(dev, (dev + 1) % 8) for dev in range(8)])  30.6 us
    all_gather x1, waiting for transfers between devices, per_device(): hidden_full = lax.all_gather(hidden_part, 'dp', axis=1, tiled=True)  27.8 us
  transfers between devices with their start and end apart: 15, of which 14 were waited for; matrix products, arithmetic and copies ran while one was open for 27% of the time, Pallas kernels for 0%

profile of v1, /device:TPU:2, one launch (start us, length us, event | category | flops | bytes accessed | tf_op | source)
XLA Modules:
  0.0 698.2 jit_solution(5718206393414813421)
XLA Ops:
  7.2 2.4 reshape_reshape.24
  12.2 2.0 maximum_bitcast_fusion
  14.7 3.8 reduce.10
  18.4 5.4 reshape.303
  23.9 11.8 %all-to-all-start.1 = ((bf16[32,2,24576]{2,1,0:T(2,128)(2,1)}), bf16[32,2,24576]{2,1,0:T(2,128)(2,1)S(1)}, u32[]{:S(2)}, u32[]{:S(2)}) async-start(bf16[32,2,24576]{2,1,0:T(2,128)(2,1)} %reshape.303), calls=%async_computation.1 | async-start | bytes 6291456 | tf_op jit(solution)/shard_map/all_to_all | solution.py:63
  36.0 2.7 reshape_reshape.30
  38.7 2.7 reshape_reshape.31
  42.8 1.4 dynamic-update-slice.1
  44.2 1.4 dynamic-update-slice.2
  45.6 9.3 %dynamic-update-slice.3 = f32[32,32771]{1,0:T(8,128)} dynamic-update-slice(f32[32,32771]{1,0:T(8,128)} %dynamic-update-slice.2, f32[32,16384]{1,0:T(8,128)} %reshape_reshape.30, s32[]{} %constant.178, s32[]{} %constant.181) | dynamic-update-slice | bytes 4194308
  54.9 8.6 %dynamic-update-slice.4 = f32[32,32771]{1,0:T(8,128)} dynamic-update-slice(f32[32,32771]{1,0:T(8,128)} %dynamic-update-slice.3, f32[32,16384]{1,0:T(8,128)} %reshape_reshape.31, s32[]{} %constant.178, s32[]{} %constant.182) | dynamic-update-slice | bytes 4194308 | tf_op jit(solution)/shard_map/concatenate | solution.py:46
  63.5 9.8 %all_to_all.43 = f32[32,1,32771]{2,1,0:T(1,128)} reshape(f32[32,32771]{1,0:T(8,128)} %dynamic-update-slice.4) | data formatting | bytes 8389376 | tf_op jit(solution)/shard_map/all_to_all | solution.py:72
  73.5 33.4 %all-to-all-done.1 = bf16[32,2,24576]{2,1,0:T(2,128)(2,1)S(1)} async-done(((bf16[32,2,24576]{2,1,0:T(2,128)(2,1)}), bf16[32,2,24576]{2,1,0:T(2,128)(2,1)S(1)}, u32[]{:S(2)}, u32[]{:S(2)}) %all-to-all-start.1) | async-done | bytes 3145760 | tf_op jit(solution)/shard_map/all_to_all | solution.py:63
  106.9 7.8 %all-to-all-start.3 = ((f32[32,1,32771]{2,1,0:T(1,128)}), f32[32,1,32771]{2,1,0:T(1,128)}, u32[]{:S(2)}, u32[]{:S(2)}) async-start(f32[32,1,32771]{2,1,0:T(1,128)} %all_to_all.43), calls=%async_computation.3 | async-start | bytes 8421376 | tf_op jit(solution)/shard_map/all_to_all | solution.py:72
  114.7 12.5 %reshape.304 = bf16[32,1,49152]{2,1,0:T(2,128)(2,1)} reshape(bf16[32,2,24576]{2,1,0:T(2,128)(2,1)S(1)} %all-to-all-done.1) | data formatting | bytes 6291456
  127.2 6.2 copy.83
  133.5 4.3 gather_fusion.1
  137.8 2.3 bitcast_select_fusion.1
  140.0 3.7 reduce.11
  143.8 5.4 reshape.305
  149.2 59.0 %all-to-all-done.3 = f32[32,1,32771]{2,1,0:T(1,128)} async-done(((f32[32,1,32771]{2,1,0:T(1,128)}), f32[32,1,32771]{2,1,0:T(1,128)}, u32[]{:S(2)}, u32[]{:S(2)}) %all-to-all-start.3) | async-done | bytes 4194720 | tf_op jit(solution)/shard_map/all_to_all | solution.py:72
  208.1 8.3 %all-to-all-start.2 = ((bf16[32,2,24576]{2,1,0:T(2,128)(2,1)}), bf16[32,2,24576]{2,1,0:T(2,128)(2,1)}, u32[]{:S(2)}, u32[]{:S(2)}) async-start(bf16[32,2,24576]{2,1,0:T(2,128)(2,1)} %reshape.305), calls=%async_computation.2 | async-start | bytes 6291456 | tf_op jit(solution)/shard_map/all_to_all | solution.py:64
  216.5 4.4 copy.81
  220.9 7.6 %gather_fusion.2 = f32[32,32771]{1,0:T(8,128)} fusion(f32[32,32771]{1,0:T(8,128)} %bitcast.77, s32[1024]{0:T(1024)S(1)} %pad_clamp_fusion.1), kind=kCustom, calls=%fused_computation.2 | custom fusion | bytes 8389504 | tf_op jit(solution)/shard_map/jit(_take)/gather | solution.py:74
  228.5 2.5 bitcast_select_fusion
  231.1 6.3 copy.60
  237.3 50.3 %all-to-all-done.2 = bf16[32,2,24576]{2,1,0:T(2,128)(2,1)} async-done(((bf16[32,2,24576]{2,1,0:T(2,128)(2,1)}), bf16[32,2,24576]{2,1,0:T(2,128)(2,1)}, u32[]{:S(2)}, u32[]{:S(2)}) %all-to-all-start.2) | async-done | bytes 3145760 | tf_op jit(solution)/shard_map/all_to_all | solution.py:64
  287.6 7.4 %all-to-all-start.4 = ((f32[32,1,32771]{2,1,0:T(1,128)}), f32[32,1,32771]{2,1,0:T(1,128)}, u32[]{:S(2)}, u32[]{:S(2)}) async-start(f32[32,1,32771]{2,1,0:T(1,128)} %copy.60), calls=%async_computation.4 | async-start | bytes 8421376 | tf_op jit(solution)/shard_map/all_to_all | solution.py:73
  295.3 5.0 collective-permute-done
  300.3 1.7 reduce-window.6
  302.0 3.5 collective-permute-done.1
  305.8 5.0 collective-permute-done.2
  310.9 5.1 collective-permute-done.3
  316.1 3.6 scatter_custom_fusion
  319.6 1.7 collective-permute-done.4
  321.3 5.2 collective-permute-done.5
  326.7 5.1 collective-permute-done.6
  332.1 7.8 %gather_fusion = bf16[1024,4096]{1,0:T(8,128)(2,1)} fusion(bf16[96,4096]{1,0:T(8,128)(2,1)S(1)} %constant_dynamic-slice_fusion, s32[1024]{0:T(1024)S(1)} %get-tuple-element.17), kind=kCustom, calls=%fused_computation | custom fusion | bytes 16781312 | tf_op jit(solution)/shard_map/jit(_take)/gather | solution.py:140
  339.9 7.4 %broadcast_select_fusion = bf16[32,32,4096]{2,1,0:T(8,128)(2,1)} fusion(bf16[32,32,4096]{2,1,0:T(8,128)(2,1)} %bitcast.80, pred[32,32]{1,0:T(8,128)(4,1)S(1)} %broadcast_in_dim.103), kind=kLoop, calls=%fused_computation.7 | loop fusion | flops 4194304 | bytes 16778240 | tf_op jit(solution)/shard_map/jit(_take)/select_n | solution.py:140
  347.3 41.3 %all-to-all-done.4 = f32[32,1,32771]{2,1,0:T(1,128)} async-done(((f32[32,1,32771]{2,1,0:T(1,128)}), f32[32,1,32771]{2,1,0:T(1,128)}, u32[]{:S(2)}, u32[]{:S(2)}) %all-to-all-start.4) | async-done | bytes 4194720 | tf_op jit(solution)/shard_map/all_to_all | solution.py:73
  388.7 7.6 %all-to-all-start = ((bf16[32,32,4096]{2,1,0:T(8,128)(2,1)}), bf16[32,32,4096]{2,1,0:T(8,128)(2,1)}, u32[]{:S(2)}, u32[]{:S(2)}) async-start(bf16[32,32,4096]{2,1,0:T(8,128)(2,1)} %broadcast_select_fusion), calls=%async_computation | async-start | bytes 16777216 | tf_op jit(solution)/shard_map/all_to_all | solution.py:142
  396.6 4.5 gather_fusion.4
  401.2 4.0 gather_fusion.5
  406.6 18.9 %reshape.306 = bf16[32,1,49152]{2,1,0:T(2,128)(2,1)} reshape(bf16[32,2,24576]{2,1,0:T(2,128)(2,1)} %all-to-all-done.2) | data formatting | bytes 6291456
  425.5 6.2 copy.82
  431.7 2.5 copy.80
  434.4 2.1 multiply_convert_fusion.2
  436.8 2.3 convert_element_type.66
  439.1 2.3 convert_element_type.69
  441.5 145.2 %all-to-all-done = bf16[32,32,4096]{2,1,0:T(8,128)(2,1)} async-done(((bf16[32,32,4096]{2,1,0:T(8,128)(2,1)}), bf16[32,32,4096]{2,1,0:T(8,128)(2,1)}, u32[]{:S(2)}, u32[]{:S(2)}) %all-to-all-start) | async-done | bytes 8388640 | tf_op jit(solution)/shard_map/all_to_all | solution.py:142
  586.6 13.2 %all-to-all-start.6 = ((bf16[32,32,512]{2,1,0:T(8,128)(2,1)}), bf16[32,32,512]{2,1,0:T(8,128)(2,1)}, u32[]{:S(2)}, u32[]{:S(2)}) async-start(bf16[32,32,512]{2,1,0:T(8,128)(2,1)} %multiply_convert_fusion), calls=%async_computation.6 | async-start | bytes 2097152 | tf_op jit(solution)/shard_map/all_to_all | solution.py:143
  600.1 6.0 fusion.15
  606.1 6.4 fusion.1
  612.6 1.5 slice_convert_fusion
  614.0 1.7 reshape.234
  615.9 27.8 %all-gather.2.cloned.1.call-done = bf16[1024,1024]{1,0:T(8,128)(2,1)} async-done(((bf16[1024,128]{1,0:T(8,128)(2,1)}), bf16[1024,1024]{1,0:T(8,128)(2,1)}) %all-gather.2.cloned.1.call-update) | async-done | bytes 2097168 | tf_op jit(solution)/shard_map/all_gather | solution.py:154
  646.3 2.3 convolution_convert_fusion
  648.5 10.1 %all-to-all-start.5 = ((bf16[32,32,512]{2,1,0:T(8,128)(2,1)}), bf16[32,32,512]{2,1,0:T(8,128)(2,1)S(1)}, u32[]{:S(2)}, u32[]{:S(2)}) async-start(bf16[32,32,512]{2,1,0:T(8,128)(2,1)} %bitcast.12), calls=%async_computation.5 | async-start | bytes 2097152 | tf_op jit(solution)/shard_map/all_to_all | solution.py:160
  658.7 4.7 slice_multiply_fusion
  663.4 2.7 mul.143
  666.1 1.5 mul.150
  667.6 9.3 %fusion.5 = (f32[1,1024,512]{2,1,0:T(8,128)}, bf16[1,1024,512]{2,1,0:T(8,128)(2,1)}, f32[1,1024,512]{2,1,0:T(8,128)}) fusion(f32[1024,512]{1,0:T(8,128)} %mul.150, f32[1024,512]{1,0:T(8,128)} %mul.143, f32[1024,512]{1,0:T(8,128)} %copy-done.3, f32[128,8,4,128]{3,2,1,0:T(4,128)} %bitcast.87, bf16[1024,1024]{1,0:T(8,128)(2,1)} %all-gather.2.cloned.1.call-done, ...), kind=kOutput, calls=%fused_computation.34 | convolution fusion | flops 1081606144 | bytes 16777216 | tf_op jit(solution)/shard_map/dot_general | solution.py:156
  677.0 10.2 %all-to-all-done.5 = bf16[32,32,512]{2,1,0:T(8,128)(2,1)S(1)} async-done(((bf16[32,32,512]{2,1,0:T(8,128)(2,1)}), bf16[32,32,512]{2,1,0:T(8,128)(2,1)S(1)}, u32[]{:S(2)}, u32[]{:S(2)}) %all-to-all-start.5) | async-done | bytes 1048608 | tf_op jit(solution)/shard_map/all_to_all | solution.py:160
  687.2 2.7 gather_fusion.3
  (98 shorter events, 12.3 us)
Async XLA Ops:
  7.2 394.1 %copy-start = (bf16[96,512]{1,0:T(8,128)(2,1)S(1)}, bf16[96,512]{1,0:T(8,128)(2,1)}, u32[]{:S(2)}) copy-start(bf16[96,512]{1,0:T(8,128)(2,1)} %param.17) | copy-start | bytes 294916
  7.2 2.5 copy-start.4
  7.2 3.7 copy-start.5
  23.9 11.8 %copy-start.11 = (f32[1,32,1]{1,2,0:T(1,128)S(1)}, f32[1,32,1]{1,2,0:T(1,128)}, u32[]{:S(2)}) copy-start(f32[1,32,1]{1,2,0:T(1,128)} %param.20) | copy-start | bytes 388
  23.9 11.9 %copy-start.12 = (f32[1,32,1]{1,2,0:T(1,128)S(1)}, f32[1,32,1]{1,2,0:T(1,128)}, u32[]{:S(2)}) copy-start(f32[1,32,1]{1,2,0:T(1,128)} %param.21) | copy-start | bytes 388
  23.9 12.0 %copy-start.10 = (f32[1,8,4]{1,2,0:T(4,128)S(1)}, f32[1,8,4]{1,2,0:T(4,128)}, u32[]{:S(2)}) copy-start(f32[1,8,4]{1,2,0:T(4,128)} %param.23) | copy-start | bytes 388
  23.9 83.0 %all-to-all-start.1 = ((bf16[32,2,24576]{2,1,0:T(2,128)(2,1)}), bf16[32,2,24576]{2,1,0:T(2,128)(2,1)S(1)}, u32[]{:S(2)}, u32[]{:S(2)}) async-start(bf16[32,2,24576]{2,1,0:T(2,128)(2,1)} %reshape.303), calls=%async_computation.1 | async-start | bytes 6291456 | tf_op jit(solution)/shard_map/all_to_all | solution.py:63
  63.5 9.8 %copy-start.13 = (s32[32]{0:T(128)S(1)}, s32[32]{0:T(128)}, u32[]{:S(2)}) copy-start(s32[32]{0:T(128)} %param.27) | copy-start | bytes 388
  63.5 9.8 %copy-start.14 = (s32[32]{0:T(128)S(1)}, s32[32]{0:T(128)}, u32[]{:S(2)}) copy-start(s32[32]{0:T(128)} %param.26) | copy-start | bytes 388
  106.9 101.2 %all-to-all-start.3 = ((f32[32,1,32771]{2,1,0:T(1,128)}), f32[32,1,32771]{2,1,0:T(1,128)}, u32[]{:S(2)}, u32[]{:S(2)}) async-start(f32[32,1,32771]{2,1,0:T(1,128)} %all_to_all.43), calls=%async_computation.3 | async-start | bytes 8421376 | tf_op jit(solution)/shard_map/all_to_all | solution.py:72
  208.1 79.5 %all-to-all-start.2 = ((bf16[32,2,24576]{2,1,0:T(2,128)(2,1)}), bf16[32,2,24576]{2,1,0:T(2,128)(2,1)}, u32[]{:S(2)}, u32[]{:S(2)}) async-start(bf16[32,2,24576]{2,1,0:T(2,128)(2,1)} %reshape.305), calls=%async_computation.2 | async-start | bytes 6291456 | tf_op jit(solution)/shard_map/all_to_all | solution.py:64
  237.3 57.7 %copy-start.7 = (bf16[96,512]{1,0:T(8,128)(2,1)S(1)}, bf16[96,512]{1,0:T(8,128)(2,1)}, u32[]{:S(2)}) copy-start(bf16[96,512]{1,0:T(8,128)(2,1)} %param.14) | copy-start | bytes 294916
  237.3 57.7 %copy-start.8 = (s32[96,8]{0,1:T(8,128)S(1)}, s32[96,8]{0,1:T(8,128)}, u32[]{:S(2)}) copy-start(s32[96,8]{0,1:T(8,128)} %param.16) | copy-start | bytes 9220
  287.6 101.0 %all-to-all-start.4 = ((f32[32,1,32771]{2,1,0:T(1,128)}), f32[32,1,32771]{2,1,0:T(1,128)}, u32[]{:S(2)}, u32[]{:S(2)}) async-start(f32[32,1,32771]{2,1,0:T(1,128)} %copy.60), calls=%async_computation.4 | async-start | bytes 8421376 | tf_op jit(solution)/shard_map/all_to_all | solution.py:73
  295.0 5.3 collective-permute-start
  300.3 5.3 collective-permute-start.1
  305.5 5.3 collective-permute-start.2
  310.8 5.3 collective-permute-start.3
  316.0 5.3 collective-permute-start.4
  321.3 5.3 collective-permute-start.5
  326.6 5.3 collective-permute-start.6
  347.3 49.1 %copy-start.9 = (f32[96,8]{0,1:T(8,128)S(1)}, f32[96,8]{0,1:T(8,128)}, u32[]{:S(2)}) copy-start(f32[96,8]{0,1:T(8,128)} %param.15) | copy-start | bytes 9220
  388.7 198.0 %all-to-all-start = ((bf16[32,32,4096]{2,1,0:T(8,128)(2,1)}), bf16[32,32,4096]{2,1,0:T(8,128)(2,1)}, u32[]{:S(2)}, u32[]{:S(2)}) async-start(bf16[32,32,4096]{2,1,0:T(8,128)(2,1)} %broadcast_select_fusion), calls=%async_computation | async-start | bytes 16777216 | tf_op jit(solution)/shard_map/all_to_all | solution.py:142
  434.2 2.6 copy-start.1
  586.6 61.9 %all-to-all-start.6 = ((bf16[32,32,512]{2,1,0:T(8,128)(2,1)}), bf16[32,32,512]{2,1,0:T(8,128)(2,1)}, u32[]{:S(2)}, u32[]{:S(2)}) async-start(bf16[32,32,512]{2,1,0:T(8,128)(2,1)} %multiply_convert_fusion), calls=%async_computation.6 | async-start | bytes 2097152 | tf_op jit(solution)/shard_map/all_to_all | solution.py:143
  599.8 43.9 %all-gather.2.cloned.1.call-start = ((), (), s32[]{:S(2)}) async-start(), calls=%async_computation.7 | async-start | bytes 2359296 | tf_op jit(solution)/shard_map/all_gather | solution.py:154
  600.1 6.0 copy-start.6
  615.8 32.8 %copy-start.3 = (f32[1024,512]{1,0:T(8,128)}, f32[1024,512]{1,0:T(8,128)S(1)}, u32[]{:S(2)}) copy-start(f32[1024,512]{1,0:T(8,128)S(1)} %reshape.234) | copy-start | bytes 6291460
  643.7 2.6 copy-start.15
  644.9 1.3 copy-start.2
  648.5 38.6 %all-to-all-start.5 = ((bf16[32,32,512]{2,1,0:T(8,128)(2,1)}), bf16[32,32,512]{2,1,0:T(8,128)(2,1)S(1)}, u32[]{:S(2)}, u32[]{:S(2)}) async-start(bf16[32,32,512]{2,1,0:T(8,128)(2,1)} %bitcast.12), calls=%async_computation.5 | async-start | bytes 2097152 | tf_op jit(solution)/shard_map/all_to_all | solution.py:160
Sparse Core Ops, SparseCore 0:
  612.7 30.9 all-gather.1
